TPU v7x, 512 devices: a whole 4x8x8 slice. The times are simulated.
512 devices in a mesh: hours: 64 (over z, x, core), region: 8 (over y).
Axes of the slice: x: 4, y: 8, z: 8, core: 2. Of those that a mesh axis runs over, the one named last changes fastest.
Arguments:
- availability: float32 [4096, 16, 1024], P('hours', None, 'region'), may hold values from 0.1 to 1
- demand: float32 [4096, 1024], P('hours', 'region'), may hold values from 2 to 72, as said below
- gen_cost: float32 [16, 1024], P(None, 'region'), may hold values from 0.05 to 1
- cap_cost: float32 [8, 2048], P('region', 'hours'), may hold values from 204.8 to 2048
- owner_map: int32 [8, 2048], P('region'), may hold values from 0 to 2047, each once within a row
- line_ends: int32 [2, 2048], P(None, 'region'), may hold values from 0 to 127
- line_limit: float32 [2048], P('region'), may hold values from 0.5 to 4
- cross_ends: int32 [2, 8, 256], P(None, 'region'), may hold values from 0 to 127
- cross_limit: float32 [8, 256], P('region'), may hold values from 0.5 to 4
- pair_counts: int32 [8, 8], P('region'), may hold values from 0 to 32, as said below
- store_node: int32 [2048], P('region'), may hold values from 0 to 127
- store_energy: float32 [2048], P('region'), may hold values from 0.02 to 0.4
- store_power: float32 [2048], P('region'), may hold values from 0.2 to 2
- price_start: float32 [4096, 1024], P('hours', 'region'), may hold values from -3 to 0.5
Outputs:
- dispatch: float32 [4096, 16, 1024], P('hours', None, 'region')
- capacity: float32 [8, 2048], P('region', 'hours')
- prices: float32 [4096, 1024], P('hours', 'region')
- charge_state: float32 [4096, 2048], P('hours', 'region')
Inputs may be any that keep to these rules, and one draw needn't show every extreme that they name: `demand`: loads are positive. `owner_map`: each row lists every capacity column of its region once. `pair_counts`: cross lines in use among the 32 slots of each ordered pair of regions; a region has none to itself; some pair uses all 32.
All inputs are finite; a program needn't handle non-finite values.
Results may differ from a plain program's by a relative error of at most 0.00018.
Values sent between devices are 32-bit elements; how exact they have to be, the bound alone decides.
A program may use at most 64 MiB of HBM per device.

v0:
```python
import jax
import jax.numpy as jnp
from jax import lax
from jax.sharding import PartitionSpec as P

ITERS = 4
epsilon = 1e-06
highest = lax.Precision.HIGHEST


def shifted(value, axis, steps):
    count = lax.axis_size(axis)
    pairs = [(source, (source + steps) % count) for source in range(count)]
    return lax.ppermute(value, axis, pairs)


def one_hot(indices, labels):
    return (indices[:, None] == labels[None, :]).astype(jnp.float32)


def to_owners(partial_value, owned_cols):
    summed = lax.psum(partial_value, "hours")
    return lax.dynamic_slice_in_dim(summed, lax.axis_index("hours") * owned_cols, owned_cols)


def spread_columns(capacity_bar):
    return lax.all_gather(capacity_bar, "hours", axis=0, tiled=True)


def body(
    availability,
    demand,
    gen_cost,
    cap_cost,
    owner_map,
    line_ends,
    line_limit,
    cross_ends,
    cross_limit,
    pair_counts,
    store_node,
    store_energy,
    store_power,
    price_start,
):
    hour_rows, tech_count, node_count = availability.shape
    region_count = lax.axis_size("region")
    slot_count = cross_limit.shape[1]
    slot_width = slot_count // region_count
    owned_cols = cap_cost.shape[1]
    owner_cols = owner_map[0]
    inverse = jnp.argsort(owner_cols)
    node_ids = jnp.arange(node_count, dtype=jnp.int32)
    line_inc = one_hot(line_ends[1], node_ids) - one_hot(line_ends[0], node_ids)
    store_map = one_hot(store_node, node_ids)
    leave_map = one_hot(cross_ends[0, 0], node_ids)
    slot_ids = jnp.arange(slot_count, dtype=jnp.int32)
    pair_of = slot_ids // slot_width
    region_ids = jnp.arange(region_count, dtype=jnp.int32)
    in_use = jnp.sum(
        jnp.where(pair_of[:, None] == region_ids[None, :], pair_counts[0][None, :], 0), axis=1
    )
    cross_bound = jnp.where(slot_ids % slot_width < in_use, cross_limit[0], 0.0)
    reach_map = one_hot(
        pair_of * node_count + cross_ends[1, 0],
        jnp.arange(region_count * node_count, dtype=jnp.int32),
    )
    column_costs = cap_cost[0]
    col_weight = to_owners(jnp.sum(availability, axis=0).reshape(-1)[owner_cols], owned_cols)
    dispatch = jnp.zeros_like(availability)
    capacity = jnp.zeros((owned_cols,), jnp.float32)
    inner_flow = jnp.zeros((hour_rows, line_limit.shape[0]), jnp.float32)
    cross_flow = jnp.zeros((hour_rows, slot_count), jnp.float32)
    mirror_flow = jnp.zeros((hour_rows, slot_count), jnp.float32)
    discharge = jnp.zeros((hour_rows, store_node.shape[0]), jnp.float32)
    charge = jnp.zeros((hour_rows, store_node.shape[0]), jnp.float32)
    prices = price_start
    cap_duals = jnp.zeros_like(availability)
    store_duals = jnp.zeros((hour_rows, store_node.shape[0]), jnp.float32)
    weight = jnp.float32(1.0)
    for iteration in range(ITERS):
        final_sweep = iteration == ITERS - 1
        primal_step = 0.5 / weight
        far_side = jnp.dot(
            lax.all_gather(prices, "region", axis=1, tiled=True), reach_map.T, precision=highest
        )
        if iteration == 0:
            next_duals = jnp.zeros_like(store_duals)
            cap_pull = jnp.zeros((owned_cols,), jnp.float32)
        else:
            next_row = shifted(store_duals[:1], "hours", -1)
            next_duals = jnp.concatenate([store_duals[1:], next_row], axis=0)
            cap_pull = to_owners(
                jnp.sum(availability * cap_duals, axis=0).reshape(-1)[owner_cols], owned_cols
            )
        dispatch_new = jnp.maximum(
            dispatch - primal_step * (gen_cost[None] + prices[:, None, :] + cap_duals), 0.0
        )
        capacity_new = jnp.maximum(
            capacity - (column_costs - cap_pull) / (weight * col_weight), 0.0
        )
        inner_new = jnp.clip(
            inner_flow - primal_step * jnp.dot(prices, line_inc.T, precision=highest),
            -line_limit,
            line_limit,
        )
        cross_new = jnp.clip(
            cross_flow - primal_step * (far_side - jnp.dot(prices, leave_map.T, precision=highest)),
            -cross_bound,
            cross_bound,
        )
        mirror_new = mirror_flow
        discharge_new = jnp.clip(
            discharge
            - primal_step * (jnp.dot(prices, store_map.T, precision=highest) + store_duals),
            -store_power,
            store_power,
        )
        charge_new = jnp.clip(charge - primal_step * (store_duals - next_duals), 0.0, store_energy)
        if not final_sweep:
            cap_change = capacity_new - capacity
            primal_sq = (
                jnp.sum((dispatch_new - dispatch) ** 2)
                + jnp.sum(cap_change**2)
                + jnp.sum((inner_new - inner_flow) ** 2)
                + jnp.sum((cross_new - cross_flow) ** 2)
                + jnp.sum((discharge_new - discharge) ** 2)
                + jnp.sum((charge_new - charge) ** 2)
            )
            primal_sum = lax.psum(primal_sq, ("hours", "region"))
        dispatch_bar = 2.0 * dispatch_new - dispatch
        capacity_bar = 2.0 * capacity_new - capacity
        inner_bar = 2.0 * inner_new - inner_flow
        cross_bar = 2.0 * cross_new - cross_flow
        discharge_bar = 2.0 * discharge_new - discharge
        charge_bar = 2.0 * charge_new - charge
        capacity_all = spread_columns(capacity_bar)
        cap_dense = capacity_all[inverse].reshape(tech_count, node_count)
        per_dest = jnp.dot(cross_bar, reach_map, precision=highest)
        balance = (
            jnp.sum(dispatch_bar, axis=1)
            + jnp.dot(inner_bar, line_inc, precision=highest)
            + (
                lax.psum_scatter(per_dest, "region", scatter_dimension=1, tiled=True)
                - jnp.dot(cross_bar, leave_map, precision=highest)
            )
            + jnp.dot(discharge_bar, store_map, precision=highest)
            - demand
        )
        prev_row = shifted(charge_bar[-1:], "hours", 1)
        storage_rows = (
            charge_bar - jnp.concatenate([prev_row, charge_bar[:-1]], axis=0) + discharge_bar
        )
        cap_rows = dispatch_bar - availability * cap_dense[None]
        prices_new = prices + weight / (tech_count + 8.0) * balance
        cap_new = jnp.maximum(cap_duals + weight / 2.0 * cap_rows, 0.0)
        store_new = store_duals + weight / 3.0 * storage_rows
        if not final_sweep:
            dual_sq = (
                jnp.sum((prices_new - prices) ** 2)
                + jnp.sum((cap_new - cap_duals) ** 2)
                + jnp.sum((store_new - store_duals) ** 2)
            )
            dual_sum = lax.psum(dual_sq, ("hours", "region"))
            weight = jnp.sqrt(weight * jnp.sqrt((dual_sum + epsilon) / (primal_sum + epsilon)))
        dispatch, capacity, inner_flow, cross_flow = (
            dispatch_new,
            capacity_new,
            inner_new,
            cross_new,
        )
        mirror_flow = mirror_new
        discharge, charge = (discharge_new, charge_new)
        prices, cap_duals, store_duals = (prices_new, cap_new, store_new)
    return (dispatch, capacity[None], prices, charge)


def solution(mesh):
    placed = (
        P("hours", None, "region"),
        P("hours", "region"),
        P(None, "region"),
        P("region", "hours"),
        P("region", None),
        P(None, "region"),
        P("region"),
        P(None, "region", None),
        P("region", None),
        P("region", None),
        P("region"),
        P("region"),
        P("region"),
        P("hours", "region"),
    )
    return jax.shard_map(
        body,
        mesh=mesh,
        in_specs=placed,
        out_specs=(
            P("hours", None, "region"),
            P("region", "hours"),
            P("hours", "region"),
            P("hours", "region"),
        ),
        check_vma=False,
    )
```

profile of v0, /device:TPU:2, one launch (start us, length us, event | category | flops | bytes accessed | tf_op | source)
XLA Modules:
  0.0 1496.5 jit_solution(16780039333863139814)
XLA Ops:
  7.9 2.0 collective-permute-start
  10.0 26.6 %all_gather.21 = f32[64,1024]{1,0:T(8,128)S(1)} all-gather(f32[64,128]{1,0:T(8,128)} %param.27), channel_id=1, replica_groups=mesh['hours'=64,'region'=8] {'region'}, dimensions={1}, use_global_device_ids=true | all-gather | bytes 294912 | tf_op jit(solution)/shard_map/all_gather | solution.py:85
  39.0 1.3 fusion.74
  41.2 11.8 gather_fusion
  53.0 126.8 %psum.70 = f32[2048]{0:T(1024)S(1)} all-reduce(f32[2048]{0:T(1024)S(1)} %gather_fusion), channel_id=1, replica_groups=mesh['hours'=64,'region'=8] {'hours'}, use_global_device_ids=true, to_apply=%region_5.6 | all-reduce | flops 2048 | bytes 16384 | tf_op jit(solution)/shard_map/psum | solution.py:22
  179.7 1.3 dynamic-slice
  182.5 126.4 %all-reduce = f32[2048]{0:T(1024)S(1)} all-reduce(f32[2048]{0:T(1024)S(1)} %multiply_dynamic-update-slice_fusion), channel_id=1, replica_groups=mesh['hours'=64,'region'=8] {'hours'}, use_global_device_ids=true, to_apply=%add | all-reduce | flops 2048 | bytes 16384
  308.9 5.0 sort.17
  314.0 11.8 gather_fusion.1
  325.8 1.1 multiply_reduce_fusion.6
  326.8 11.8 gather_fusion.2
  338.6 1.0 multiply_reduce_fusion.21
  340.6 126.1 %psum.73 = f32[2048]{0:T(1024)S(1)} all-reduce(f32[2048]{0:T(1024)S(1)} %gather_fusion.2), channel_id=1, replica_groups=mesh['hours'=64,'region'=8] {'hours'}, use_global_device_ids=true, to_apply=%region_21.22 | all-reduce | flops 2048 | bytes 16384 | tf_op jit(solution)/shard_map/psum | solution.py:22
  472.2 1.0 fusion.67
  476.0 7.0 collective-permute-start.1
  483.0 95.3 %all-reduce.5 = (f32[]{:T(128)}, f32[]{:T(128)}) all-reduce(f32[]{:T(128)S(6)} %add.309, f32[]{:T(128)S(6)} %add.315), channel_id=1, replica_groups=mesh['hours'=64,'region'=8] {'hours','region'}, use_global_device_ids=true, to_apply=%region_9.10 | all-reduce | flops 2 | bytes 16 | tf_op jit(solution)/shard_map/psum | solution.py:164
  579.7 24.8 %all_gather.23 = f32[64,1024]{1,0:T(8,128)S(1)} all-gather(f32[64,128]{1,0:T(8,128)S(1)} %get-tuple-element.56), channel_id=1, replica_groups=mesh['hours'=64,'region'=8] {'region'}, dimensions={1}, use_global_device_ids=true | all-gather | bytes 294912 | tf_op jit(solution)/shard_map/all_gather | solution.py:85
  604.5 1.0 multiply_reduce_fusion.17
  606.4 120.4 %all-reduce.1 = f32[2048]{0:T(1024)S(1)} all-reduce(f32[2048]{0:T(1024)S(1)} %subtract_dynamic-update-slice_fusion.1), channel_id=1, replica_groups=mesh['hours'=64,'region'=8] {'hours'}, use_global_device_ids=true, to_apply=%add.1 | all-reduce | flops 2048 | bytes 16384
  726.8 11.8 gather_fusion.3
  740.7 0.9 multiply_reduce_fusion.16
  741.6 1.3 fusion.72
  742.9 1.2 multiply_reduce_fusion.3
  744.2 11.8 gather_fusion.4
  756.0 1.9 collective-permute-start.2
  758.2 131.1 %psum.76 = f32[2048]{0:T(1024)S(1)} all-reduce(f32[2048]{0:T(1024)S(1)} %gather_fusion.4), channel_id=1, replica_groups=mesh['hours'=64,'region'=8] {'hours'}, use_global_device_ids=true, to_apply=%region_36.37 | all-reduce | flops 2048 | bytes 16384 | tf_op jit(solution)/shard_map/psum | solution.py:22
  891.9 1.0 multiply_reduce_fusion.15
  894.2 1.0 fusion.63
  898.0 1.9 collective-permute-start.3
  900.0 100.8 %all-reduce.4 = (f32[]{:T(128)}, f32[]{:T(128)}) all-reduce(f32[]{:T(128)S(6)} %add.329, f32[]{:T(128)S(6)} %add.335), channel_id=1, replica_groups=mesh['hours'=64,'region'=8] {'hours','region'}, use_global_device_ids=true, to_apply=%region_24.25 | all-reduce | flops 2 | bytes 16 | tf_op jit(solution)/shard_map/psum | solution.py:164
  1002.9 1.0 multiply_reduce_fusion.12
  1003.9 24.8 %all_gather.25 = f32[64,1024]{1,0:T(8,128)S(1)} all-gather(f32[64,128]{1,0:T(8,128)S(1)} %get-tuple-element.63), channel_id=1, replica_groups=mesh['hours'=64,'region'=8] {'region'}, dimensions={1}, use_global_device_ids=true | all-gather | bytes 294912 | tf_op jit(solution)/shard_map/all_gather | solution.py:85
  1029.5 120.4 %all-reduce.2 = f32[2048]{0:T(1024)S(1)} all-reduce(f32[2048]{0:T(1024)S(1)} %subtract_dynamic-update-slice_fusion), channel_id=1, replica_groups=mesh['hours'=64,'region'=8] {'hours'}, use_global_device_ids=true, to_apply=%add.2 | all-reduce | flops 2048 | bytes 16384
  1149.9 11.8 gather_fusion.5
  1161.7 1.9 collective-permute-start.4
  1164.4 0.9 multiply_reduce_fusion.11
  1165.3 1.3 fusion.70
  1166.7 1.4 multiply_reduce_fusion
  1168.1 11.8 gather_fusion.6
  1180.2 131.1 %psum.79 = f32[2048]{0:T(1024)S(1)} all-reduce(f32[2048]{0:T(1024)S(1)} %gather_fusion.6), channel_id=1, replica_groups=mesh['hours'=64,'region'=8] {'hours'}, use_global_device_ids=true, to_apply=%region_48.49 | all-reduce | flops 2048 | bytes 16384 | tf_op jit(solution)/shard_map/psum | solution.py:22
  1316.2 1.0 fusion.59
  1320.0 1.9 collective-permute-start.5
  1321.9 100.9 %all-reduce.3 = (f32[]{:T(128)}, f32[]{:T(128)}) all-reduce(f32[]{:T(128)S(6)} %add.349, f32[]{:T(128)S(6)} %add.355), channel_id=1, replica_groups=mesh['hours'=64,'region'=8] {'hours','region'}, use_global_device_ids=true, to_apply=%region_39.40 | all-reduce | flops 2 | bytes 16 | tf_op jit(solution)/shard_map/psum | solution.py:164
  1424.3 24.8 %all_gather.27 = f32[64,1024]{1,0:T(8,128)S(1)} all-gather(f32[64,128]{1,0:T(8,128)S(1)} %get-tuple-element.70), channel_id=1, replica_groups=mesh['hours'=64,'region'=8] {'region'}, dimensions={1}, use_global_device_ids=true | all-gather | bytes 294912 | tf_op jit(solution)/shard_map/all_gather | solution.py:85
  1449.5 1.6 subtract_reduce_fusion
  1452.1 1.3 fusion.68
  1455.2 32.9 %reduce-scatter.11.cloned.1.call-done = f32[64,128]{1,0:T(8,128)} async-done(((f32[64,1024]{1,0:T(8,128)}), f32[64,128]{1,0:T(8,128)}) %reduce-scatter.11.cloned.1.call-update) | async-done | bytes 32784 | tf_op jit(solution)/shard_map/reduce_scatter | solution.py:144
  1488.1 1.0 fusion.55
  (102 shorter events, 20.9 us)
Async XLA Ops:
  7.2 465.0 %reduce-scatter.5.cloned.1.call-start = ((), (), s32[]{:S(2)}) async-start(), calls=%async_computation.4 | async-start | bytes 294912 | tf_op jit(solution)/shard_map/reduce_scatter | solution.py:144
  7.9 2.1 copy-start.9
  7.9 461.4 %collective-permute-start = (f32[1,256]{1,0:T(1,128)S(1)}, f32[1,256]{1,0:T(1,128)S(1)}, u32[]{:S(2)}, u32[]{:S(2)}) collective-permute-start(f32[1,256]{1,0:T(1,128)S(1)} %bitcast.122), channel_id=1, source_target_pairs={{0,8},{8,16},{16,24},{24,32},{32,40},{40,48},{48,56},{56,64},{64,7... | collective-permute-start | bytes 3080 | tf_op jit(solution)/shard_map/ppermute | solution.py:14
  36.6 0.7 copy-start.13
  36.6 0.7 copy-start.12
  37.2 0.8 copy-start.1
  37.3 3.8 copy-start
  40.3 853.9 %reduce-scatter.7.cloned.1.call-start = ((), (), s32[]{:S(2)}) async-start(), calls=%async_computation.5 | async-start | bytes 294912 | tf_op jit(solution)/shard_map/reduce_scatter | solution.py:144
  40.3 0.7 copy-start.11
  40.3 0.7 copy-start.5
  40.4 0.7 copy-start.10
  181.0 0.7 copy-start.8
  314.0 11.8 copy-start.3
  340.6 126.1 %copy-start.7 = (f32[256]{0:T(256)S(1)}, f32[256]{0:T(256)}, u32[]{:S(2)}) copy-start(f32[256]{0:T(256)} %param.26) | copy-start | bytes 3076
  469.2 0.7 copy-start.4
  472.1 1.1 copy-start.2
  476.0 262.6 %collective-permute-start.1 = (f32[1,256]{1,0:T(1,128)S(1)}, f32[1,256]{1,0:T(1,128)S(1)}, u32[]{:S(2)}, u32[]{:S(2)}) collective-permute-start(f32[1,256]{1,0:T(1,128)S(1)} %slice.79), channel_id=1, source_target_pairs={{0,504},{8,0},{16,8},{24,16},{32,24},{40,32},{48,40},{56,48},{64,5... | collective-permute-start | bytes 3080 | tf_op jit(solution)/shard_map/ppermute | solution.py:14
  738.6 0.7 copy-start.6
  742.9 573.2 %reduce-scatter.9.cloned.1.call-start = ((), (), s32[]{:S(2)}) async-start(), calls=%async_computation.6 | async-start | bytes 294912 | tf_op jit(solution)/shard_map/reduce_scatter | solution.py:144
  756.0 135.9 %collective-permute-start.2 = (f32[1,256]{1,0:T(1,128)S(1)}, f32[1,256]{1,0:T(1,128)S(1)}, u32[]{:S(2)}, u32[]{:S(2)}) collective-permute-start(f32[1,256]{1,0:T(1,128)S(1)} %slice.80), channel_id=1, source_target_pairs={{0,8},{8,16},{16,24},{24,32},{32,40},{40,48},{48,56},{56,64},{64,7... | collective-permute-start | bytes 3080 | tf_op jit(solution)/shard_map/ppermute | solution.py:14
  898.0 130.7 %collective-permute-start.3 = (f32[1,256]{1,0:T(1,128)S(1)}, f32[1,256]{1,0:T(1,128)S(1)}, u32[]{:S(2)}, u32[]{:S(2)}) collective-permute-start(f32[1,256]{1,0:T(1,128)S(1)} %slice.83), channel_id=1, source_target_pairs={{0,504},{8,0},{16,8},{24,16},{32,24},{40,32},{48,40},{56,48},{64,5... | collective-permute-start | bytes 3080 | tf_op jit(solution)/shard_map/ppermute | solution.py:14
  1161.7 152.2 %collective-permute-start.4 = (f32[1,256]{1,0:T(1,128)S(1)}, f32[1,256]{1,0:T(1,128)S(1)}, u32[]{:S(2)}, u32[]{:S(2)}) collective-permute-start(f32[1,256]{1,0:T(1,128)S(1)} %slice.84), channel_id=1, source_target_pairs={{0,8},{8,16},{16,24},{24,32},{32,40},{40,48},{48,56},{56,64},{64,7... | collective-permute-start | bytes 3080 | tf_op jit(solution)/shard_map/ppermute | solution.py:14
  1166.6 321.5 %reduce-scatter.11.cloned.1.call-start = ((), (), s32[]{:S(2)}) async-start(), calls=%async_computation.7 | async-start | bytes 294912 | tf_op jit(solution)/shard_map/reduce_scatter | solution.py:144
  1320.0 134.3 %collective-permute-start.5 = (f32[1,256]{1,0:T(1,128)S(1)}, f32[1,256]{1,0:T(1,128)S(1)}, u32[]{:S(2)}, u32[]{:S(2)}) collective-permute-start(f32[1,256]{1,0:T(1,128)S(1)} %slice.87), channel_id=1, source_target_pairs={{0,504},{8,0},{16,8},{24,16},{32,24},{40,32},{48,40},{56,48},{64,5... | collective-permute-start | bytes 3080 | tf_op jit(solution)/shard_map/ppermute | solution.py:14
Sparse Core Ops, SparseCore 0:
  40.4 42.1 reduce-scatter.4
  743.0 39.1 reduce-scatter.6
  1166.7 41.5 reduce-scatter.8
  1453.5 34.5 reduce-scatter.10
where the time goes:
time: 1500 us
  blocking collectives  1280 us (85%)
  local copies, waits for them, and re-layouts  86.5 us (6%)
  between operations  36.6 us (2%)
  waiting for transfers between devices  33 us (2%)
  matrix products  26.5 us (2%)
  starting transfers between devices  16.8 us (1%)
  other arithmetic  16.8 us (1%)
    psum x4, blocking collectives, to_owners(): summed = lax.psum(partial_value, 'hours')  515 us
    unnamed x3, blocking collectives  367 us
    psum x3, blocking collectives, body(): dual_sum = lax.psum(dual_sq, ('hours', 'region'))  297 us
    all_gather x4, blocking collectives, body(): lax.all_gather(prices, 'region', axis=1, tiled=True)  101 us
    gather x3, local copies, waits for them, and re-layouts, body(): cap_dense = capacity_all[inverse].reshape(tech_count, node_count)  35.3 us
    gather x3, local copies, waits for them, and re-layouts, body(): jnp.sum(availability * cap_duals, axis=0).reshape(-1)[owner_cols]  35.3 us
    reduce_scatter x4, waiting for transfers between devices, body(): lax.psum_scatter(per_dest, 'region', scatter_dimension=1, tiled=True)  32.9 us
  transfers between devices with their start and end apart: 10, of which 1 were waited for; matrix products, arithmetic and copies ran while one was open for 7% of the time, Pallas kernels for 0%

commit v1 on v0

--- a/solution.py
+++ b/solution.py
@@ -161,7 +161,7 @@
                 + jnp.sum((cap_new - cap_duals) ** 2)
                 + jnp.sum((store_new - store_duals) ** 2)
             )
-            dual_sum = lax.psum(dual_sq, ("hours", "region"))
+            dual_sum = jnp.sum(lax.all_gather(dual_sq, ("hours", "region")), axis=0)
             weight = jnp.sqrt(weight * jnp.sqrt((dual_sum + epsilon) / (primal_sum + epsilon)))
         dispatch, capacity, inner_flow, cross_flow = (
             dispatch_new,

time: 1500 us -> 1500 us (level)
    psum x3 -> x0, blocking collectives: 297 us -> none  [body(): dual_sum = lax.psum(dual_sq, ('hours', 'region'))]
    unnamed x3 -> x6, blocking collectives: 367 us -> 664 us
where the time goes in v1:
time: 1500 us
  blocking collectives  1280 us (85%)
  local copies, waits for them, and re-layouts  86.8 us (6%)
  between operations  36.6 us (2%)
  waiting for transfers between devices  32.9 us (2%)
  matrix products  26.5 us (2%)
  other arithmetic  18.6 us (1%)
  starting transfers between devices  16.8 us (1%)
    unnamed x6, blocking collectives  664 us
    psum x4, blocking collectives, to_owners(): summed = lax.psum(partial_value, 'hours')  515 us
    all_gather x4, blocking collectives, body(): lax.all_gather(prices, 'region', axis=1, tiled=True)  101 us
    gather x3, local copies, waits for them, and re-layouts, body(): cap_dense = capacity_all[inverse].reshape(tech_count, node_count)  35.3 us
    gather x3, local copies, waits for them, and re-layouts, body(): jnp.sum(availability * cap_duals, axis=0).reshape(-1)[owner_cols]  35.3 us
    reduce_scatter x4, waiting for transfers between devices, body(): lax.psum_scatter(per_dest, 'region', scatter_dimension=1, tiled=True)  32.8 us
  transfers between devices with their start and end apart: 10, of which 1 were waited for; matrix products, arithmetic and copies ran while one was open for 7% of the time, Pallas kernels for 0%

profile of v1, /device:TPU:2, one launch (start us, length us, event | category | flops | bytes accessed | tf_op | source)
XLA Modules:
  0.0 1498.5 jit_solution(12454229993629076851)
XLA Ops:
  7.9 2.0 collective-permute-start
  10.0 26.6 %all_gather.39 = f32[64,1024]{1,0:T(8,128)S(1)} all-gather(f32[64,128]{1,0:T(8,128)} %param.27), channel_id=1, replica_groups=mesh['hours'=64,'region'=8] {'region'}, dimensions={1}, use_global_device_ids=true | all-gather | bytes 294912 | tf_op jit(solution)/shard_map/all_gather | solution.py:85
  39.0 1.3 fusion.74
  41.2 11.8 gather_fusion
  53.0 126.8 %psum.49 = f32[2048]{0:T(1024)S(1)} all-reduce(f32[2048]{0:T(1024)S(1)} %gather_fusion), channel_id=1, replica_groups=mesh['hours'=64,'region'=8] {'hours'}, use_global_device_ids=true, to_apply=%region_5.6 | all-reduce | flops 2048 | bytes 16384 | tf_op jit(solution)/shard_map/psum | solution.py:22
  179.7 1.3 dynamic-slice
  182.5 126.4 %all-reduce = f32[2048]{0:T(1024)S(1)} all-reduce(f32[2048]{0:T(1024)S(1)} %multiply_dynamic-update-slice_fusion), channel_id=1, replica_groups=mesh['hours'=64,'region'=8] {'hours'}, use_global_device_ids=true, to_apply=%add | all-reduce | flops 2048 | bytes 16384
  308.9 5.0 sort.17
  314.0 11.8 gather_fusion.1
  325.8 1.1 multiply_reduce_fusion.6
  326.8 11.8 gather_fusion.2
  338.6 1.0 multiply_reduce_fusion.21
  340.6 126.1 %psum.51 = f32[2048]{0:T(1024)S(1)} all-reduce(f32[2048]{0:T(1024)S(1)} %gather_fusion.2), channel_id=1, replica_groups=mesh['hours'=64,'region'=8] {'hours'}, use_global_device_ids=true, to_apply=%region_21.22 | all-reduce | flops 2048 | bytes 16384 | tf_op jit(solution)/shard_map/psum | solution.py:22
  470.9 7.0 collective-permute-start.1
  479.1 1.0 fusion.67
  483.1 95.2 %all-reduce.8 = (f32[512]{0:T(512)S(1)}, f32[]{:T(128)}) all-reduce(f32[512]{0:T(512)S(1)} %dynamic-update-slice.1, f32[]{:T(128)S(6)} %add.309), channel_id=1, replica_groups=mesh['hours'=64,'region'=8] {'hours','region'}, use_global_device_ids=true, to_apply=%add.1 | all-reduce | flops 513 | bytes 4104
  580.4 24.8 %all_gather.43 = f32[64,1024]{1,0:T(8,128)S(1)} all-gather(f32[64,128]{1,0:T(8,128)S(1)} %get-tuple-element.56), channel_id=1, replica_groups=mesh['hours'=64,'region'=8] {'region'}, dimensions={1}, use_global_device_ids=true | all-gather | bytes 294912 | tf_op jit(solution)/shard_map/all_gather | solution.py:85
  605.2 1.0 multiply_reduce_fusion.17
  607.0 120.4 %all-reduce.2 = f32[2048]{0:T(1024)S(1)} all-reduce(f32[2048]{0:T(1024)S(1)} %subtract_dynamic-update-slice_fusion.1), channel_id=1, replica_groups=mesh['hours'=64,'region'=8] {'hours'}, use_global_device_ids=true, to_apply=%add.2 | all-reduce | flops 2048 | bytes 16384
  727.5 11.8 gather_fusion.3
  741.4 0.9 multiply_reduce_fusion.16
  742.3 1.3 fusion.72
  743.6 1.2 multiply_reduce_fusion.3
  744.9 11.8 gather_fusion.4
  756.7 1.9 collective-permute-start.2
  758.9 131.1 %psum.53 = f32[2048]{0:T(1024)S(1)} all-reduce(f32[2048]{0:T(1024)S(1)} %gather_fusion.4), channel_id=1, replica_groups=mesh['hours'=64,'region'=8] {'hours'}, use_global_device_ids=true, to_apply=%region_36.37 | all-reduce | flops 2048 | bytes 16384 | tf_op jit(solution)/shard_map/psum | solution.py:22
  892.6 1.0 multiply_reduce_fusion.15
  893.6 1.9 collective-permute-start.3
  896.8 1.0 fusion.63
  900.8 100.7 %all-reduce.7 = (f32[512]{0:T(512)S(1)}, f32[]{:T(128)}) all-reduce(f32[512]{0:T(512)S(1)} %dynamic-update-slice.3, f32[]{:T(128)S(6)} %add.329), channel_id=1, replica_groups=mesh['hours'=64,'region'=8] {'hours','region'}, use_global_device_ids=true, to_apply=%add.3 | all-reduce | flops 513 | bytes 4104
  1004.2 1.0 multiply_reduce_fusion.12
  1005.3 24.8 %all_gather.47 = f32[64,1024]{1,0:T(8,128)S(1)} all-gather(f32[64,128]{1,0:T(8,128)S(1)} %get-tuple-element.63), channel_id=1, replica_groups=mesh['hours'=64,'region'=8] {'region'}, dimensions={1}, use_global_device_ids=true | all-gather | bytes 294912 | tf_op jit(solution)/shard_map/all_gather | solution.py:85
  1030.9 120.4 %all-reduce.4 = f32[2048]{0:T(1024)S(1)} all-reduce(f32[2048]{0:T(1024)S(1)} %subtract_dynamic-update-slice_fusion), channel_id=1, replica_groups=mesh['hours'=64,'region'=8] {'hours'}, use_global_device_ids=true, to_apply=%add.4 | all-reduce | flops 2048 | bytes 16384
  1151.3 11.8 gather_fusion.5
  1163.1 1.9 collective-permute-start.4
  1165.7 0.9 multiply_reduce_fusion.11
  1166.7 1.3 fusion.70
  1168.0 1.4 multiply_reduce_fusion
  1169.5 11.8 gather_fusion.6
  1181.6 131.1 %psum.55 = f32[2048]{0:T(1024)S(1)} all-reduce(f32[2048]{0:T(1024)S(1)} %gather_fusion.6), channel_id=1, replica_groups=mesh['hours'=64,'region'=8] {'hours'}, use_global_device_ids=true, to_apply=%region_48.49 | all-reduce | flops 2048 | bytes 16384 | tf_op jit(solution)/shard_map/psum | solution.py:22
  1316.2 1.9 collective-permute-start.5
  1319.4 1.0 fusion.59
  1323.4 100.9 %all-reduce.6 = (f32[512]{0:T(512)S(1)}, f32[]{:T(128)}) all-reduce(f32[512]{0:T(512)S(1)} %dynamic-update-slice.5, f32[]{:T(128)S(6)} %add.349), channel_id=1, replica_groups=mesh['hours'=64,'region'=8] {'hours','region'}, use_global_device_ids=true, to_apply=%add.5 | all-reduce | flops 513 | bytes 4104
  1426.4 24.8 %all_gather.51 = f32[64,1024]{1,0:T(8,128)S(1)} all-gather(f32[64,128]{1,0:T(8,128)S(1)} %get-tuple-element.70), channel_id=1, replica_groups=mesh['hours'=64,'region'=8] {'region'}, dimensions={1}, use_global_device_ids=true | all-gather | bytes 294912 | tf_op jit(solution)/shard_map/all_gather | solution.py:85
  1451.6 1.6 subtract_reduce_fusion
  1454.1 1.3 fusion.68
  1457.3 32.8 %reduce-scatter.11.cloned.1.call-done = f32[64,128]{1,0:T(8,128)} async-done(((f32[64,1024]{1,0:T(8,128)}), f32[64,128]{1,0:T(8,128)}) %reduce-scatter.11.cloned.1.call-update) | async-done | bytes 32784 | tf_op jit(solution)/shard_map/reduce_scatter | solution.py:144
  1490.1 1.0 fusion.55
  (111 shorter events, 23.1 us)
Async XLA Ops:
  7.2 472.0 %reduce-scatter.5.cloned.1.call-start = ((), (), s32[]{:S(2)}) async-start(), calls=%async_computation.4 | async-start | bytes 294912 | tf_op jit(solution)/shard_map/reduce_scatter | solution.py:144
  7.9 2.1 copy-start.9
  7.9 461.4 %collective-permute-start = (f32[1,256]{1,0:T(1,128)S(1)}, f32[1,256]{1,0:T(1,128)S(1)}, u32[]{:S(2)}, u32[]{:S(2)}) collective-permute-start(f32[1,256]{1,0:T(1,128)S(1)} %bitcast.125), channel_id=1, source_target_pairs={{0,8},{8,16},{16,24},{24,32},{32,40},{40,48},{48,56},{56,64},{64,7... | collective-permute-start | bytes 3080 | tf_op jit(solution)/shard_map/ppermute | solution.py:14
  36.6 0.7 copy-start.13
  36.6 0.7 copy-start.12
  37.2 0.8 copy-start.1
  37.3 3.8 copy-start
  40.3 856.5 %reduce-scatter.7.cloned.1.call-start = ((), (), s32[]{:S(2)}) async-start(), calls=%async_computation.5 | async-start | bytes 294912 | tf_op jit(solution)/shard_map/reduce_scatter | solution.py:144
  40.3 0.7 copy-start.11
  40.3 0.7 copy-start.5
  40.4 0.7 copy-start.10
  181.0 0.7 copy-start.8
  314.0 11.8 copy-start.3
  340.6 126.1 %copy-start.7 = (f32[256]{0:T(256)S(1)}, f32[256]{0:T(256)}, u32[]{:S(2)}) copy-start(f32[256]{0:T(256)} %param.26) | copy-start | bytes 3076
  469.2 0.7 copy-start.4
  470.9 268.4 %collective-permute-start.1 = (f32[1,256]{1,0:T(1,128)S(1)}, f32[1,256]{1,0:T(1,128)S(1)}, u32[]{:S(2)}, u32[]{:S(2)}) collective-permute-start(f32[1,256]{1,0:T(1,128)S(1)} %slice.79), channel_id=1, source_target_pairs={{0,504},{8,0},{16,8},{24,16},{32,24},{40,32},{48,40},{56,48},{64,5... | collective-permute-start | bytes 3080 | tf_op jit(solution)/shard_map/ppermute | solution.py:14
  479.1 1.1 copy-start.2
  739.3 0.7 copy-start.6
  743.6 575.8 %reduce-scatter.9.cloned.1.call-start = ((), (), s32[]{:S(2)}) async-start(), calls=%async_computation.6 | async-start | bytes 294912 | tf_op jit(solution)/shard_map/reduce_scatter | solution.py:144
  756.7 135.9 %collective-permute-start.2 = (f32[1,256]{1,0:T(1,128)S(1)}, f32[1,256]{1,0:T(1,128)S(1)}, u32[]{:S(2)}, u32[]{:S(2)}) collective-permute-start(f32[1,256]{1,0:T(1,128)S(1)} %slice.80), channel_id=1, source_target_pairs={{0,8},{8,16},{16,24},{24,32},{32,40},{40,48},{48,56},{56,64},{64,7... | collective-permute-start | bytes 3080 | tf_op jit(solution)/shard_map/ppermute | solution.py:14
  893.6 136.5 %collective-permute-start.3 = (f32[1,256]{1,0:T(1,128)S(1)}, f32[1,256]{1,0:T(1,128)S(1)}, u32[]{:S(2)}, u32[]{:S(2)}) collective-permute-start(f32[1,256]{1,0:T(1,128)S(1)} %slice.83), channel_id=1, source_target_pairs={{0,504},{8,0},{16,8},{24,16},{32,24},{40,32},{48,40},{56,48},{64,5... | collective-permute-start | bytes 3080 | tf_op jit(solution)/shard_map/ppermute | solution.py:14
  1163.1 152.2 %collective-permute-start.4 = (f32[1,256]{1,0:T(1,128)S(1)}, f32[1,256]{1,0:T(1,128)S(1)}, u32[]{:S(2)}, u32[]{:S(2)}) collective-permute-start(f32[1,256]{1,0:T(1,128)S(1)} %slice.84), channel_id=1, source_target_pairs={{0,8},{8,16},{16,24},{24,32},{32,40},{40,48},{48,56},{56,64},{64,7... | collective-permute-start | bytes 3080 | tf_op jit(solution)/shard_map/ppermute | solution.py:14
  1168.0 322.1 %reduce-scatter.11.cloned.1.call-start = ((), (), s32[]{:S(2)}) async-start(), calls=%async_computation.7 | async-start | bytes 294912 | tf_op jit(solution)/shard_map/reduce_scatter | solution.py:144
  1316.2 140.2 %collective-permute-start.5 = (f32[1,256]{1,0:T(1,128)S(1)}, f32[1,256]{1,0:T(1,128)S(1)}, u32[]{:S(2)}, u32[]{:S(2)}) collective-permute-start(f32[1,256]{1,0:T(1,128)S(1)} %slice.87), channel_id=1, source_target_pairs={{0,504},{8,0},{16,8},{24,16},{32,24},{40,32},{48,40},{56,48},{64,5... | collective-permute-start | bytes 3080 | tf_op jit(solution)/shard_map/ppermute | solution.py:14
Sparse Core Ops, SparseCore 0:
  40.4 42.1 reduce-scatter.4
  743.7 39.1 reduce-scatter.6
  1168.1 41.4 reduce-scatter.8
  1455.6 34.4 reduce-scatter.10
